TPU v7x, 32 devices: a whole 2x2x4 slice. The times are simulated.
32 devices in a mesh: batch: 4 (over z), seq: 2 (over x), head: 4 (over y, core).
Axes of the slice: x: 2, y: 2, z: 4, core: 2. Of those that a mesh axis runs over, the one named last changes fastest.
Arguments:
- queries: bfloat16 [5120, 8192], P(('batch', 'seq', 'head')), parts along dimension 0, may hold values from -6 to 6
- keys: bfloat16 [5120, 8192], P(('batch', 'seq', 'head')), parts along dimension 0, may hold values from -6 to 6
- values: bfloat16 [5120, 8192], P(('batch', 'seq', 'head')), parts along dimension 0, may hold values from -6 to 6
- group_order: int32 [8, 2], P(('batch', 'seq')), parts along dimension 0, may hold values from 0 to 3, as said below
- gain: float32 [8192], P('head'), may hold values from 0.1 to 1.9
Outputs:
- attended: bfloat16 [5120, 8192], P(('batch', 'seq'), 'head'), parts along dimension 0
There are 4 independent parts, one for each index of `batch`. A program takes and returns all parts, laid end to end along the dimension named above; an argument that names none is the same for every part. Nothing has to cross between parts.
Inputs may be any that keep to these rules, and one draw needn't show every extreme that they name: `group_order`: row d holds d and 3 - d, in either order.
All inputs are finite; a program needn't handle non-finite values.
Results may differ from a plain program's by a relative error of at most 0.01.
Values may be sent and summed in bfloat16 or wider, within the bound.
A program may use at most 64 MiB of HBM per device.

v0:
```python
import jax
import jax.numpy as jnp
from jax import lax
from jax.sharding import PartitionSpec as P

DH = 128


def local(queries, keys, values, group_order, gain):
    q_all, k_all, v_all = (
        lax.all_to_all(queries, "head", split_axis=1, concat_axis=0, tiled=True),
        lax.all_to_all(keys, "head", split_axis=1, concat_axis=0, tiled=True),
        lax.all_to_all(values, "head", split_axis=1, concat_axis=0, tiled=True),
    )
    rows = q_all.shape[0]
    half = rows // 2
    local_heads = gain.shape[0] // DH
    pairs = lax.axis_size("seq")
    here = lax.axis_index("seq")
    qx = q_all.reshape(rows, local_heads, DH)
    kx = k_all.reshape(rows, local_heads, DH)
    vx = v_all.reshape(rows, local_heads, DH)
    kh = kx.reshape(2, half, local_heads, DH)
    vh = vx.reshape(2, half, local_heads, DH)
    state = jnp.einsum("jthd,jthe->jhde", kh, vh, preferred_element_type=jnp.float32).astype(
        jnp.bfloat16
    )
    state = lax.optimization_barrier(state).astype(jnp.float32)
    order = group_order[0]
    low_first = order[0] < pairs
    lows = jnp.where(low_first, state[0], state[1])
    highs = jnp.where(low_first, state[1], state[0])
    empty = jnp.zeros_like(lows)
    low_sum = empty
    high_sum = empty
    piece_low = lax.all_gather(lows[None].astype(jnp.bfloat16), "seq", axis=0, tiled=True).astype(
        jnp.float32
    )
    piece_high = lax.all_gather(highs[None].astype(jnp.bfloat16), "seq", axis=0, tiled=True).astype(
        jnp.float32
    )
    owners = jnp.arange(piece_low.shape[0], dtype=jnp.int32)
    below = (owners < here).astype(jnp.float32)[:, None, None, None]
    other = (owners != here).astype(jnp.float32)[:, None, None, None]
    above = (owners > here).astype(jnp.float32)[:, None, None, None]
    low_sum = low_sum + jnp.sum(piece_low * below, axis=0)
    high_sum = high_sum + jnp.sum(piece_low * other + piece_high * above, axis=0)
    first_pre = jnp.where(low_first, low_sum, high_sum).astype(jnp.bfloat16)
    second_pre = jnp.where(low_first, high_sum, low_sum).astype(jnp.bfloat16)
    index = jnp.arange(rows, dtype=jnp.int32)
    position = order[index // half] * half + index % half
    scores = jnp.einsum("thd,shd->hts", qx, kx, preferred_element_type=jnp.float32)
    allowed = position[:, None] >= position[None, :]
    scores = jnp.where(allowed[None], scores, 0.0).astype(jnp.bfloat16)
    intra = jnp.einsum("hts,she->the", scores, vx, preferred_element_type=jnp.float32)
    qh = qx.reshape(2, half, local_heads, DH)
    first_term = jnp.einsum("thd,hde->the", qh[0], first_pre, preferred_element_type=jnp.float32)
    second_term = jnp.einsum("thd,hde->the", qh[1], second_pre, preferred_element_type=jnp.float32)
    raw = intra + jnp.concatenate([first_term, second_term], axis=0)
    scale = lax.rsqrt(jnp.mean(raw * raw, axis=-1, keepdims=True) + 1e-06)
    gains = gain.reshape(local_heads, DH)
    return (raw * scale * gains).astype(jnp.bfloat16).reshape(rows, local_heads * DH)


def solution(mesh):
    return jax.shard_map(
        local,
        mesh=mesh,
        in_specs=(
            P(("batch", "seq", "head"), None),
            P(("batch", "seq", "head"), None),
            P(("batch", "seq", "head"), None),
            P(("batch", "seq"), None),
            P("head"),
        ),
        out_specs=P(("batch", "seq"), "head"),
        check_vma=False,
    )
```

profile of v0, /device:TPU:0, one launch (start us, length us, event | category | flops | bytes accessed | tf_op | source)
XLA Modules:
  0.0 172.7 jit_solution(8265969338175430533)
XLA Ops:
  6.5 3.6 %copy.84 = bf16[20,4,8,2048]{3,2,0,1:T(8,128)(2,1)} copy(bf16[20,4,8,2048]{3,2,1,0:T(8,128)(2,1)} %bitcast.61) | data formatting | bytes 5242880 | tf_op jit(solution)/shard_map/all_to_all | solution.py:12
  10.1 4.2 %all-to-all-start.1 = ((bf16[160,4,2048]{2,0,1:T(8,128)(2,1)}), bf16[160,4,2048]{2,0,1:T(8,128)(2,1)S(1)}, u32[]{:S(2)}, u32[]{:S(2)}) async-start(bf16[160,4,2048]{2,0,1:T(8,128)(2,1)} %bitcast.55), calls=%async_computation.1 | async-start | bytes 5242880 | tf_op jit(solution)/shard_map/all_to_all | solution.py:12
  14.3 3.6 %copy.83 = bf16[20,4,8,2048]{3,2,0,1:T(8,128)(2,1)} copy(bf16[20,4,8,2048]{3,2,1,0:T(8,128)(2,1)} %bitcast.62) | data formatting | bytes 5242880 | tf_op jit(solution)/shard_map/all_to_all | solution.py:13
  17.9 27.8 %all-to-all-done.1 = bf16[160,4,2048]{2,0,1:T(8,128)(2,1)S(1)} async-done(((bf16[160,4,2048]{2,0,1:T(8,128)(2,1)}), bf16[160,4,2048]{2,0,1:T(8,128)(2,1)S(1)}, u32[]{:S(2)}, u32[]{:S(2)}) %all-to-all-start.1) | async-done | bytes 2621472 | tf_op jit(solution)/shard_map/all_to_all | solution.py:12
  45.7 1.5 copy-done.1
  47.2 3.7 %all-to-all-start.2 = ((bf16[160,4,2048]{2,0,1:T(8,128)(2,1)}), bf16[160,4,2048]{2,0,1:T(8,128)(2,1)S(1)}, u32[]{:S(2)}, u32[]{:S(2)}) async-start(bf16[160,4,2048]{2,0,1:T(8,128)(2,1)} %bitcast.54), calls=%async_computation.2 | async-start | bytes 5242880 | tf_op jit(solution)/shard_map/all_to_all | solution.py:13
  50.9 3.7 %copy.85 = bf16[20,4,8,2048]{3,2,0,1:T(8,128)(2,1)} copy(bf16[20,4,8,2048]{3,2,1,0:T(8,128)(2,1)} %bitcast.63) | data formatting | bytes 5242880 | tf_op jit(solution)/shard_map/all_to_all | solution.py:11
  54.6 0.6 fusion.37
  55.8 2.4 %copy.40 = bf16[80,8,16,128]{3,2,1,0:T(8,128)(2,1)} copy(bf16[80,8,16,128]{3,1,2,0:T(8,128)(2,1)S(1)} %bitcast.53) | data formatting | bytes 5242880
  58.3 23.9 %all-to-all-done.2 = bf16[160,4,2048]{2,0,1:T(8,128)(2,1)S(1)} async-done(((bf16[160,4,2048]{2,0,1:T(8,128)(2,1)}), bf16[160,4,2048]{2,0,1:T(8,128)(2,1)S(1)}, u32[]{:S(2)}, u32[]{:S(2)}) %all-to-all-start.2) | async-done | bytes 2621472 | tf_op jit(solution)/shard_map/all_to_all | solution.py:13
  82.1 1.5 copy-done
  83.6 3.7 %all-to-all-start = ((bf16[160,4,2048]{2,0,1:T(8,128)(2,1)}), bf16[160,4,2048]{2,0,1:T(8,128)(2,1)S(1)}, u32[]{:S(2)}, u32[]{:S(2)}) async-start(bf16[160,4,2048]{2,0,1:T(8,128)(2,1)} %bitcast.51), calls=%async_computation | async-start | bytes 5242880 | tf_op jit(solution)/shard_map/all_to_all | solution.py:11
  87.3 0.0 all-gather.5.cloned.1.call-start
  87.4 2.7 %copy.41 = bf16[80,8,16,128]{3,2,1,0:T(8,128)(2,1)S(1)} copy(bf16[80,8,16,128]{3,1,2,0:T(8,128)(2,1)} %bitcast.52) | data formatting | bytes 5242880
  90.1 2.1 %fusion.20 = bf16[2,16,128,128]{3,2,1,0:T(8,128)(2,1)S(1)} fusion(bf16[2,320,16,128]{3,2,1,0:T(8,128)(2,1)S(1)} %bitcast.66, bf16[2,320,16,128]{3,2,1,0:T(8,128)(2,1)S(1)} %bitcast.65), kind=kOutput, calls=%fused_computation.21 | convolution fusion | flops 336068608 | bytes 6291456 | tf_op jit(solution)/shard_map/jthd,jthe->jhde/dot_general | solution.py:25
  92.2 1.0 select_convert_fusion.3
  93.2 0.2 all-gather.3.cloned.1.call-start
  93.5 0.5 all-gather.3.cloned.1.call-update
  94.0 1.3 fusion.34
  95.3 0.3 broadcast_compare_fusion
  95.6 23.0 %all-to-all-done = bf16[160,4,2048]{2,0,1:T(8,128)(2,1)S(1)} async-done(((bf16[160,4,2048]{2,0,1:T(8,128)(2,1)}), bf16[160,4,2048]{2,0,1:T(8,128)(2,1)S(1)}, u32[]{:S(2)}, u32[]{:S(2)}) %all-to-all-start) | async-done | bytes 2621472 | tf_op jit(solution)/shard_map/all_to_all | solution.py:11
  118.6 2.3 %copy.39 = bf16[80,8,16,128]{3,2,1,0:T(8,128)(2,1)} copy(bf16[80,8,16,128]{3,1,2,0:T(8,128)(2,1)S(1)} %bitcast.49) | data formatting | bytes 5242880
  120.9 0.3 fusion.36
  121.2 0.3 copy.44
  121.5 0.3 copy.45
  121.9 18.2 %all-gather.3.cloned.1.call-done = bf16[2,16,128,128]{3,2,1,0:T(8,128)(2,1)} async-done(((bf16[1,16,128,128]{3,2,1,0:T(8,128)(2,1)}), bf16[2,16,128,128]{3,2,1,0:T(8,128)(2,1)}) %all-gather.3.cloned.1.call-update) | async-done | bytes 1048592 | tf_op jit(solution)/shard_map/all_gather | solution.py:36
  140.1 2.2 %fusion.11 = (bf16[16,128,128]{2,1,0:T(8,128)(2,1)S(1)}, bf16[16,128,128]{2,1,0:T(8,128)(2,1)S(1)}) fusion(bf16[2,16,128,128]{3,2,1,0:T(8,128)(2,1)} %all-gather.3.cloned.1.call-done, f32[2]{0:T(128)S(1)} %compare_convert_fusion.2, f32[2]{0:T(128)S(1)} %get-tuple-element.15, bf16[2,16,128,128]{3,2,1,0:T(8,128)(2,1)} %all-gather.5.cloned.1.call-done, ...), kind=kLoop, calls=%fused_computation.16 | loop fusion | flops 3670016 | bytes 3145752 | tf_op jit(solution)/shard_map/reduce_sum | solution.py:46
  142.3 2.4 %convolution_bitcast_fusion = f32[320,16,128]{0,2,1:T(8,128)} fusion(bf16[320,16,128]{2,1,0:T(8,128)(2,1)S(1)} %bitcast.60, bf16[16,128,128]{2,1,0:T(8,128)(2,1)S(1)} %get-tuple-element.6, bf16[16,128,128]{2,1,0:T(8,128)(2,1)S(1)} %get-tuple-element.5, pred[]{:T(512)} %bitcast.6), kind=kOutput, calls=%fused_computation.19 | convolution fusion | flops 168034304 | bytes 4980737 | tf_op jit(solution)/shard_map/thd,hde->the/dot_general | solution.py:58
  144.7 2.5 %convolution_bitcast_fusion.1 = f32[320,16,128]{0,2,1:T(8,128)} fusion(bf16[320,16,128]{2,1,0:T(8,128)(2,1)S(1)} %bitcast.59, bf16[16,128,128]{2,1,0:T(8,128)(2,1)S(1)} %get-tuple-element.5, bf16[16,128,128]{2,1,0:T(8,128)(2,1)S(1)} %get-tuple-element.6, pred[]{:T(512)} %bitcast.6), kind=kOutput, calls=%fused_computation.20 | convolution fusion | flops 168034304 | bytes 4980737 | tf_op jit(solution)/shard_map/thd,hde->the/dot_general | solution.py:57
  147.2 12.8 %multiply_reduce_fusion = (f32[640,16]{0,1:T(8,128)S(1)}, f32[640,16,128]{0,2,1:T(8,128)}) fusion(f32[320,16,128]{0,2,1:T(8,128)} %convolution_bitcast_fusion, f32[320,16,128]{0,2,1:T(8,128)} %convolution_bitcast_fusion.1, bf16[640,16,128]{2,1,0:T(8,128)(2,1)} %bitcast.67, pred[640,640]{1,0:T(8,128)(4,1)S(1)} %broadcast_compare_fusion, ...), kind=kOutput, calls=%fused_computation.3 | convolution fusion | flops 3373783040 | bytes 18800640 | tf_op jit(solution)/shard_map/hts,she->the/dot_general | solution.py:55
  160.0 3.2 %multiply_convert_fusion = bf16[640,16,128]{0,2,1:T(8,128)(2,1)S(1)} fusion(f32[640,16,128]{0,2,1:T(8,128)} %get-tuple-element.14, f32[16,128]{1,0:T(8,128)S(1)} %bitcast.69, f32[640,16]{0,1:T(8,128)S(1)} %add_rsqrt_fusion), kind=kLoop, calls=%fused_computation.2 | loop fusion | flops 3932160 | bytes 7913472 | tf_op jit(solution)/shard_map/convert_element_type | solution.py:62
  163.3 2.6 %copy.33 = bf16[640,2048]{1,0:T(8,128)(2,1)} copy(bf16[640,2048]{0,1:T(8,128)(2,1)S(1)} %bitcast.56) | data formatting | bytes 5242880 | tf_op jit(solution)/shard_map/reshape | solution.py:62
  (18 shorter events, 0.1 us)
Async XLA Ops:
  10.1 35.6 %all-to-all-start.1 = ((bf16[160,4,2048]{2,0,1:T(8,128)(2,1)}), bf16[160,4,2048]{2,0,1:T(8,128)(2,1)S(1)}, u32[]{:S(2)}, u32[]{:S(2)}) async-start(bf16[160,4,2048]{2,0,1:T(8,128)(2,1)} %bitcast.55), calls=%async_computation.1 | async-start | bytes 5242880 | tf_op jit(solution)/shard_map/all_to_all | solution.py:12
  45.7 1.5 copy-start.1
  47.2 34.9 %all-to-all-start.2 = ((bf16[160,4,2048]{2,0,1:T(8,128)(2,1)}), bf16[160,4,2048]{2,0,1:T(8,128)(2,1)S(1)}, u32[]{:S(2)}, u32[]{:S(2)}) async-start(bf16[160,4,2048]{2,0,1:T(8,128)(2,1)} %bitcast.54), calls=%async_computation.2 | async-start | bytes 5242880 | tf_op jit(solution)/shard_map/all_to_all | solution.py:13
  50.8 3.7 %copy-start.6 = (s32[1,2]{1,0:T(1,128)S(1)}, s32[1,2]{1,0:T(1,128)}, u32[]{:S(2)}) copy-start(s32[1,2]{1,0:T(1,128)} %param.8) | copy-start | bytes 28
  50.9 5.0 %copy-start.2 = (bf16[160,4,2048]{2,0,1:T(8,128)(2,1)S(1)}, bf16[160,4,2048]{2,0,1:T(8,128)(2,1)}, u32[]{:S(2)}) copy-start(bf16[160,4,2048]{2,0,1:T(8,128)(2,1)} %copy-done.1) | copy-start | bytes 7864324
  82.1 1.5 copy-start
  83.6 34.9 %all-to-all-start = ((bf16[160,4,2048]{2,0,1:T(8,128)(2,1)}), bf16[160,4,2048]{2,0,1:T(8,128)(2,1)S(1)}, u32[]{:S(2)}, u32[]{:S(2)}) async-start(bf16[160,4,2048]{2,0,1:T(8,128)(2,1)} %bitcast.51), calls=%async_computation | async-start | bytes 5242880 | tf_op jit(solution)/shard_map/all_to_all | solution.py:11
  87.3 34.5 %all-gather.5.cloned.1.call-start = ((), (), s32[]{:S(2)}) async-start(), calls=%async_computation.4 | async-start | bytes 1572864 | tf_op jit(solution)/shard_map/all_gather | solution.py:39
  87.4 2.7 %copy-start.3 = (bf16[80,8,16,128]{3,2,1,0:T(8,128)(2,1)S(1)}, bf16[80,8,16,128]{3,2,1,0:T(8,128)(2,1)}, u32[]{:S(2)}) copy-start(bf16[80,8,16,128]{3,2,1,0:T(8,128)(2,1)} %copy.40) | copy-start | bytes 7864324
  90.1 2.1 %copy-start.4 = (bf16[80,8,16,128]{3,2,1,0:T(8,128)(2,1)}, bf16[80,8,16,128]{3,2,1,0:T(8,128)(2,1)S(1)}, u32[]{:S(2)}) copy-start(bf16[80,8,16,128]{3,2,1,0:T(8,128)(2,1)S(1)} %copy.41) | copy-start | bytes 7864324
  93.2 46.8 %all-gather.3.cloned.1.call-start = ((), (), s32[]{:S(2)}) async-start(), calls=%async_computation.3 | async-start | bytes 1572864 | tf_op jit(solution)/shard_map/all_gather | solution.py:36
  147.2 12.8 %copy-start.5 = (f32[2048]{0:T(1024)S(1)}, f32[2048]{0:T(1024)}, u32[]{:S(2)}) copy-start(f32[2048]{0:T(1024)} %param.9) | copy-start | bytes 24580
Sparse Core Ops, SparseCore 0:
  93.4 23.7 all-gather.4
  118.7 21.2 all-gather.2
where the time goes:
time: 173 us
  waiting for transfers between devices  93.4 us (54%)
  local copies, waits for them, and re-layouts  25.4 us (15%)
  matrix products  19.7 us (11%)
  between operations  14.2 us (8%)
  starting transfers between devices  11.8 us (7%)
  other arithmetic  8.12 us (5%)
    all_to_all x1, waiting for transfers between devices, local(): lax.all_to_all(keys, 'head', split_axis=1, concat_axis=0, tiled=True)  27.8 us
    all_to_all x1, waiting for transfers between devices, local(): lax.all_to_all(values, 'head', split_axis=1, concat_axis=0, tiled=True)  23.9 us
    all_to_all x1, waiting for transfers between devices, local(): lax.all_to_all(queries, 'head', split_axis=1, concat_axis=0, tiled=True)  23 us
    all_gather x1, waiting for transfers between devices, local(): lax.all_gather(lows[None].astype(jnp.bfloat16), 'seq', axis=0, tiled=True)  18.2 us
    dot_general x1, matrix products, local(): jnp.einsum('hts,she->the', scores, vx, preferred_element_type=jnp.float32)  12.8 us
    unnamed x19, local copies, waits for them, and re-layouts  11.1 us
    all_to_all x1, starting transfers between devices, local(): lax.all_to_all(keys, 'head', split_axis=1, concat_axis=0, tiled=True)  4.24 us
    all_to_all x1, local copies, waits for them, and re-layouts, local(): lax.all_to_all(queries, 'head', split_axis=1, concat_axis=0, tiled=True)  3.71 us
  transfers between devices with their start and end apart: 5, of which 4 were waited for; matrix products, arithmetic and copies ran while one was open for 12% of the time, Pallas kernels for 0%

commit v1 on v0

--- a/solution.py
+++ b/solution.py
@@ -1,9 +1,248 @@
 import jax
 import jax.numpy as jnp
 from jax import lax
+from jax.experimental import pallas as pl
+from jax.experimental.pallas import tpu as pltpu
 from jax.sharding import PartitionSpec as P
 
 DH = 128
+HC = 4
+LAG = 2
+MESH = pl.DeviceIdType.MESH
+F32 = jnp.float32
+BF16 = jnp.bfloat16
+
+
+def kernel(
+    q_hbm, k_hbm, v_hbm, order_ref, gain_hbm, o_hbm,
+    qb, kb, vb, raw, ob, own, oth, msg, got, gb,
+    lsem, dsend, drecv, ysend, yrecv, xsend, xrecv, osend, orecv, olocal, gsem,
+):
+    rows = q_hbm.shape[0]
+    half = 2 * rows
+    nc = qb.shape[0]
+    nh = nc // 2
+    cw = HC * DH
+    width = nh * cw
+    x = lax.axis_index("seq")
+    me = lax.axis_index("head")
+    y, c = lax.div(me, 2), lax.rem(me, 2)
+    core = {"head": y * 2 + 1 - c}
+    across = {"head": (1 - y) * 2 + c}
+    other = {"seq": 1 - x}
+
+    def columns(i, core_of):
+        late = lax.div(i, nh)
+        dest = (1 - y) * (1 - late) + y * late
+        start = (dest * 2 + core_of) * width + lax.rem(i, nh) * cw
+        return pl.ds(pl.multiple_of(start, 128), cw)
+
+    arrays = ((q_hbm, qb), (k_hbm, kb), (v_hbm, vb))
+
+    def near(a, i):
+        src, dst = arrays[a]
+        return pltpu.make_async_copy(src.at[:, columns(i, c)], dst.at[i, c], lsem.at[a, i])
+
+    def swap(a, i):
+        src, dst = arrays[a]
+        return pltpu.make_async_remote_copy(
+            src_ref=src.at[:, columns(i, 1 - c)], dst_ref=dst.at[i, c],
+            send_sem=dsend.at[a, i], recv_sem=drecv.at[a, i],
+            device_id=core, device_id_type=MESH,
+        )
+
+    def turned(j):
+        return lax.rem(j + nh, nc)
+
+    def state_copy(j):
+        return pltpu.make_async_remote_copy(
+            src_ref=own.at[turned(j)], dst_ref=oth.at[j],
+            send_sem=ysend.at[j], recv_sem=yrecv.at[j],
+            device_id=across, device_id_type=MESH,
+        )
+
+    def sum_copy(i):
+        return pltpu.make_async_remote_copy(
+            src_ref=msg.at[i], dst_ref=got.at[i],
+            send_sem=xsend.at[i], recv_sem=xrecv.at[i],
+            device_id=other, device_id_type=MESH,
+        )
+
+    my_rows = pl.ds(pl.multiple_of(y * half, 16), half)
+
+    def out_far(i):
+        return pltpu.make_async_remote_copy(
+            src_ref=ob.at[i], dst_ref=o_hbm.at[my_rows, pl.ds(pl.multiple_of(i * cw, 128), cw)],
+            send_sem=osend.at[i], recv_sem=orecv.at[i],
+            device_id=across, device_id_type=MESH,
+        )
+
+    def out_near(i):
+        return pltpu.make_async_copy(
+            ob.at[nh + i], o_hbm.at[my_rows, pl.ds(pl.multiple_of(i * cw, 128), cw)], olocal.at[i]
+        )
+
+    gain_far = pltpu.make_async_remote_copy(
+        src_ref=gain_hbm, dst_ref=gb.at[0], send_sem=gsem.at[0], recv_sem=gsem.at[1],
+        device_id=across, device_id_type=MESH,
+    )
+    gain_near = pltpu.make_async_copy(gain_hbm, gb.at[1], gsem.at[2])
+
+    barrier = pltpu.get_barrier_semaphore()
+    for partner in (core, across, other):
+        pl.semaphore_signal(barrier, inc=1, device_id=partner, device_id_type=MESH)
+
+    def begin_near(j, carry):
+        near(1, turned(j)).start()
+        near(2, turned(j)).start()
+        return carry
+
+    lax.fori_loop(0, nc, begin_near, 0)
+    gain_near.start()
+    pl.semaphore_wait(barrier, 3)
+
+    def begin_far(j, carry):
+        swap(1, turned(j)).start()
+        swap(2, turned(j)).start()
+        return carry
+
+    def begin_queries(i, carry):
+        near(0, i).start()
+        swap(0, i).start()
+        return carry
+
+    lax.fori_loop(0, nc, begin_far, 0)
+    lax.fori_loop(0, nc, begin_queries, 0)
+    gain_far.start()
+
+    row_at = lax.broadcasted_iota(jnp.int32, (half, half), 0)
+    col_at = lax.broadcasted_iota(jnp.int32, (half, half), 1)
+    allowed = row_at >= col_at
+
+    def head_of(ref, i, h):
+        return ref[i, :, :, h * DH : (h + 1) * DH].reshape(half, DH)
+
+    def states(j, carry):
+        i = turned(j)
+        for a in (1, 2):
+            near(a, i).wait()
+            swap(a, i).wait_recv()
+        for h in range(HC):
+            own[i, h] = lax.dot_general(
+                head_of(kb, i, h), head_of(vb, i, h), (((0,), (0,)), ((), ())),
+                preferred_element_type=F32,
+            ).astype(BF16)
+        state_copy(j).start()
+        return carry
+
+    lax.fori_loop(0, nc, states, 0)
+
+    mine = jnp.where(y == 0, order_ref[0, 0], order_ref[0, 1])
+    high = jnp.where(mine >= 2, 1.0, 0.0).astype(F32)
+    first = jnp.where(x == 0, 1.0, 0.0).astype(F32)
+    own_part = 1.0 - first * high
+    oth_part = 1.0 - first * (1.0 - high)
+    got_part = 1.0 - first * (1.0 - high)
+
+    def inner(i):
+        near(0, i).wait()
+        swap(0, i).wait_recv()
+        for h in range(HC):
+            scores = lax.dot_general(
+                head_of(qb, i, h), head_of(kb, i, h), (((1,), (1,)), ((), ())),
+                preferred_element_type=F32,
+            )
+            scores = jnp.where(allowed, scores, 0.0).astype(BF16)
+            raw[i, :, h * DH : (h + 1) * DH] = jnp.dot(
+                scores, head_of(vb, i, h), preferred_element_type=F32
+            )
+        state_copy(i).wait_recv()
+        msg[i] = (own_part * own[i].astype(F32) + oth_part * oth[i].astype(F32)).astype(BF16)
+        sum_copy(i).start()
+
+    def finish(i):
+        sum_copy(i).wait_recv()
+        for h in range(HC):
+            prefix = high * oth[i, h].astype(F32) + got_part * got[i, h].astype(F32)
+            total = raw[i, :, h * DH : (h + 1) * DH] + jnp.dot(
+                head_of(qb, i, h), prefix.astype(BF16), preferred_element_type=F32
+            )
+            scale = lax.rsqrt(jnp.mean(total * total, axis=-1, keepdims=True) + 1e-06)
+            gains = gb[lax.div(i, nh), pl.ds(lax.rem(i, nh) * HC + h, 1), :]
+            ob[i, :, h * DH : (h + 1) * DH] = (total * scale * gains).astype(BF16)
+
+        @pl.when(i < nh)
+        def _():
+            out_far(i).start()
+
+        @pl.when(i >= nh)
+        def _():
+            out_near(i - nh).start()
+
+    def head_step(i, carry):
+        inner(i)
+        return carry
+
+    def both_step(i, carry):
+        inner(i)
+        finish(i - LAG)
+        return carry
+
+    def tail_step(i, carry):
+        finish(i)
+        return carry
+
+    lax.fori_loop(0, LAG, head_step, 0)
+    gain_near.wait()
+    gain_far.wait()
+    lax.fori_loop(LAG, nc, both_step, 0)
+    lax.fori_loop(nc - LAG, nc, tail_step, 0)
+
+    def drain(i, carry):
+        for a in range(3):
+            swap(a, i).wait_send()
+        state_copy(i).wait_send()
+        sum_copy(i).wait_send()
+        return carry
+
+    def drain_out(i, carry):
+        out_far(i).wait()
+        out_near(i).wait()
+        return carry
+
+    lax.fori_loop(0, nc, drain, 0)
+    lax.fori_loop(0, nh, drain_out, 0)
+
+
+def fused(queries, keys, values, group_order, gain):
+    rows = queries.shape[0]
+    half = 2 * rows
+    local_heads = gain.shape[0] // DH
+    nh = local_heads // HC
+    nc = 2 * nh
+    dma = pltpu.SemaphoreType.DMA
+    anywhere = pl.BlockSpec(memory_space=pl.ANY)
+    kept = pltpu.VMEM((nc, 2, rows, HC * DH), BF16)
+    square = pltpu.VMEM((nc, HC, DH, DH), BF16)
+    return pl.pallas_call(
+        kernel,
+        out_shape=jax.ShapeDtypeStruct((2 * half, local_heads * DH), BF16),
+        in_specs=[anywhere] * 3 + [pl.BlockSpec(memory_space=pltpu.SMEM), anywhere],
+        out_specs=anywhere,
+        scratch_shapes=[
+            kept, kept, kept,
+            pltpu.VMEM((nc, half, HC * DH), F32),
+            pltpu.VMEM((nc, half, HC * DH), BF16),
+            square, square, square, square,
+            pltpu.VMEM((2, local_heads, DH), F32),
+            dma((3, nc)), dma((3, nc)), dma((3, nc)),
+            dma((nc,)), dma((nc,)), dma((nc,)), dma((nc,)),
+            dma((nh,)), dma((nh,)), dma((nh,)), dma((3,)),
+        ],
+        compiler_params=pltpu.CompilerParams(
+            collective_id=0, has_side_effects=True, vmem_limit_bytes=48 * 1024 * 1024
+        ),
+    )(queries, keys, values, group_order, gain.reshape(local_heads, DH))
 
 
 def local(queries, keys, values, group_order, gain):
@@ -63,8 +302,9 @@
 
 
 def solution(mesh):
+    small = mesh.shape["seq"] == 2 and mesh.shape["head"] == 4
     return jax.shard_map(
-        local,
+        fused if small else local,
         mesh=mesh,
         in_specs=(
             P(("batch", "seq", "head"), None),

time: 173 us -> 64.1 us (0.37)
  waiting for transfers between devices: 93.4 us -> 0 us
  Pallas kernels: 0 us -> 59.3 us
  local copies, waits for them, and re-layouts: 25.4 us -> 4.58 us
  matrix products: 19.7 us -> 0 us
  between operations: 14.2 us -> 0.01 us
  starting transfers between devices: 11.8 us -> 0 us
  other arithmetic: 8.12 us -> 0 us
    all_to_all x3 -> x0, waiting for transfers between devices: 74.6 us -> none  [the longest x1 27.8 us: local(): lax.all_to_all(keys, 'head', split_axis=1, concat_axis=0, tiled=True)]
    pallas_call x0 -> x1, Pallas kernels: none -> 59.3 us  [fused(): pl.pallas_call(kernel, out_shape=jax.ShapeDtypeStruct((2 * half, local_he...]
    dot_general x4 -> x0, matrix products: 19.7 us -> none  [the longest x1 12.8 us: local(): jnp.einsum('hts,she->the', scores, vx, preferred_element_type=jnp.float32)]
    all_gather x2 -> x0, waiting for transfers between devices: 18.2 us -> none  [the longest x1 18.2 us: local(): lax.all_gather(lows[None].astype(jnp.bfloat16), 'seq', axis=0, tiled=True)]
    all_to_all x3 -> x0, starting transfers between devices: 11.5 us -> none  [the longest x1 4.24 us: local(): lax.all_to_all(keys, 'head', split_axis=1, concat_axis=0, tiled=True)]
    all_to_all x3 -> x0, local copies, waits for them, and re-layouts: 10.8 us -> none  [the longest x1 3.71 us: local(): lax.all_to_all(queries, 'head', split_axis=1, concat_axis=0, tiled=True)]
    unnamed x19 -> x7, local copies, waits for them, and re-layouts: 11.1 us -> 4.58 us
    convert_element_type x4 -> x0, other arithmetic: 4.27 us -> none  [the longest x1 3.21 us: local(): (raw * scale * gains).astype(jnp.bfloat16).reshape(rows, local_heads * DH)]
  transfers between devices with their start and end apart: 5 -> 0, of which waited for: 4 -> 0; matrix products, arithmetic and copies ran while one was open for 12% -> 0% of each run, Pallas kernels for 0% -> 0%
where the time goes in v1:
time: 64.1 us; the launch traced here: 63.9 us
  Pallas kernels  59.3 us (93%)
  local copies, waits for them, and re-layouts  4.58 us (7%)
    pallas_call x1, Pallas kernels, fused(): pl.pallas_call(kernel, out_shape=jax.ShapeDtypeStruct((2 * half, local_he...  59.3 us
    unnamed x7, local copies, waits for them, and re-layouts  4.58 us

profile of v1, /device:TPU:0, one launch (start us, length us, event | category | flops | bytes accessed | tf_op | source)
XLA Modules:
  0.0 63.9 jit_solution(543798689520816358)
XLA Ops:
  0.0 0.0 copy-start
  0.0 1.7 %copy-done = bf16[160,8192]{1,0:T(8,128)(2,1)S(1)} copy-done((bf16[160,8192]{1,0:T(8,128)(2,1)S(1)}, bf16[160,8192]{1,0:T(8,128)(2,1)}, u32[]{:S(2)}) %copy-start) | copy-done | bytes 2621464
  1.7 0.0 copy-start.1
  1.7 0.7 %copy-done.1 = f32[2048]{0:T(1024)S(1)} copy-done((f32[2048]{0:T(1024)S(1)}, f32[2048]{0:T(1024)}, u32[]{:S(2)}) %copy-start.1) | copy-done | bytes 8216
  2.4 0.0 copy-start.2
  2.4 0.7 %copy-done.2 = s32[1,2]{1,0:T(1,128)S(1)} copy-done((s32[1,2]{1,0:T(1,128)S(1)}, s32[1,2]{1,0:T(1,128)}, u32[]{:S(2)}) %copy-start.2) | copy-done | bytes 32
  3.1 59.3 %shard_map.55 = bf16[640,2048]{1,0:T(8,128)(2,1)S(1)} custom-call(bf16[160,8192]{1,0:T(8,128)(2,1)S(1)} %copy-done, bf16[160,8192]{1,0:T(8,128)(2,1)} %k_hbm.1, bf16[160,8192]{1,0:T(8,128)(2,1)} %v_hbm.1, s32[1,2]{1,0:T(1,128)S(1)} %copy-done.2, f32[16,128]{1,0:T(8,128)S(1)} %bitcast.1), custom_call_target="tpu_custom_call" | custom-call | tf_op jit(solution)/shard_map/pallas_call | solution.py:227
  62.4 1.5 %copy.7 = bf16[640,2048]{1,0:T(8,128)(2,1)} copy(bf16[640,2048]{1,0:T(8,128)(2,1)S(1)} %shard_map.55) | data formatting | bytes 5242880
Async XLA Ops:
  0.0 1.7 %copy-start = (bf16[160,8192]{1,0:T(8,128)(2,1)S(1)}, bf16[160,8192]{1,0:T(8,128)(2,1)}, u32[]{:S(2)}) copy-start(bf16[160,8192]{1,0:T(8,128)(2,1)} %q_hbm.1) | copy-start | bytes 7864324
  1.7 0.7 %copy-start.1 = (f32[2048]{0:T(1024)S(1)}, f32[2048]{0:T(1024)}, u32[]{:S(2)}) copy-start(f32[2048]{0:T(1024)} %param.9) | copy-start | bytes 24580
  2.4 0.7 %copy-start.2 = (s32[1,2]{1,0:T(1,128)S(1)}, s32[1,2]{1,0:T(1,128)}, u32[]{:S(2)}) copy-start(s32[1,2]{1,0:T(1,128)} %order_ref.1) | copy-start | bytes 28

commit v2 on v1

--- a/solution.py
+++ b/solution.py
@@ -14,8 +14,8 @@
 
 
 def kernel(
-    q_hbm, k_hbm, v_hbm, order_ref, gain_hbm, o_hbm,
-    qb, kb, vb, raw, ob, own, oth, msg, got, gb,
+    q_hbm, k_hbm, v_hbm, order_hbm, gain_hbm, o_hbm,
+    qb, kb, vb, raw, ob, own, oth, msg, got, gb, order_ref,
     lsem, dsend, drecv, ysend, yrecv, xsend, xrecv, osend, orecv, olocal, gsem,
 ):
     rows = q_hbm.shape[0]
@@ -86,6 +86,7 @@
         src_ref=gain_hbm, dst_ref=gb.at[0], send_sem=gsem.at[0], recv_sem=gsem.at[1],
         device_id=across, device_id_type=MESH,
     )
+    order_near = pltpu.make_async_copy(order_hbm, order_ref, gsem.at[3])
     gain_near = pltpu.make_async_copy(gain_hbm, gb.at[1], gsem.at[2])
 
     barrier = pltpu.get_barrier_semaphore()
@@ -99,6 +100,7 @@
 
     lax.fori_loop(0, nc, begin_near, 0)
     gain_near.start()
+    order_near.start()
     pl.semaphore_wait(barrier, 3)
 
     def begin_far(j, carry):
@@ -137,6 +139,7 @@
 
     lax.fori_loop(0, nc, states, 0)
 
+    order_near.wait()
     mine = jnp.where(y == 0, order_ref[0, 0], order_ref[0, 1])
     high = jnp.where(mine >= 2, 1.0, 0.0).astype(F32)
     first = jnp.where(x == 0, 1.0, 0.0).astype(F32)
@@ -224,10 +227,12 @@
     anywhere = pl.BlockSpec(memory_space=pl.ANY)
     kept = pltpu.VMEM((nc, 2, rows, HC * DH), BF16)
     square = pltpu.VMEM((nc, HC, DH, DH), BF16)
+    operands = (queries, keys, values, group_order, gain.reshape(local_heads, DH))
+    stored = [pltpu.with_memory_space_constraint(a, pltpu.HBM) for a in operands]
     return pl.pallas_call(
         kernel,
         out_shape=jax.ShapeDtypeStruct((2 * half, local_heads * DH), BF16),
-        in_specs=[anywhere] * 3 + [pl.BlockSpec(memory_space=pltpu.SMEM), anywhere],
+        in_specs=[anywhere] * 5,
         out_specs=anywhere,
         scratch_shapes=[
             kept, kept, kept,
@@ -235,14 +240,15 @@
             pltpu.VMEM((nc, half, HC * DH), BF16),
             square, square, square, square,
             pltpu.VMEM((2, local_heads, DH), F32),
+            pltpu.SMEM((1, 2), jnp.int32),
             dma((3, nc)), dma((3, nc)), dma((3, nc)),
             dma((nc,)), dma((nc,)), dma((nc,)), dma((nc,)),
-            dma((nh,)), dma((nh,)), dma((nh,)), dma((3,)),
+            dma((nh,)), dma((nh,)), dma((nh,)), dma((4,)),
         ],
         compiler_params=pltpu.CompilerParams(
             collective_id=0, has_side_effects=True, vmem_limit_bytes=48 * 1024 * 1024
         ),
-    )(queries, keys, values, group_order, gain.reshape(local_heads, DH))
+    )(*stored)
 
 
 def local(queries, keys, values, group_order, gain):

time: 64.1 us -> 60.2 us (0.939)
  local copies, waits for them, and re-layouts: 4.58 us -> 1.49 us
  Pallas kernels: 59.3 us -> 58.5 us
    unnamed x7 -> x1, local copies, waits for them, and re-layouts: 4.58 us -> 1.49 us
    pallas_call x1, Pallas kernels: 59.3 us -> 58.5 us  [fused(): pl.pallas_call(kernel, out_shape=jax.ShapeDtypeStruct((2 * half, local_he...]
where the time goes in v2:
time: 60.2 us; the launch traced here: 60 us
  Pallas kernels  58.5 us (97%)
  local copies, waits for them, and re-layouts  1.49 us (2%)
    pallas_call x1, Pallas kernels, fused(): pl.pallas_call(kernel, out_shape=jax.ShapeDtypeStruct((2 * half, local_he...  58.5 us
    unnamed x1, local copies, waits for them, and re-layouts  1.49 us

profile of v2, /device:TPU:0, one launch (start us, length us, event | category | flops | bytes accessed | tf_op | source)
XLA Modules:
  0.0 60.0 jit_solution(9645542475125889299)
XLA Ops:
  0.0 58.5 %shard_map.55 = bf16[640,2048]{1,0:T(8,128)(2,1)S(1)} custom-call(bf16[160,8192]{1,0:T(8,128)(2,1)} %q_hbm.1, bf16[160,8192]{1,0:T(8,128)(2,1)} %k_hbm.1, bf16[160,8192]{1,0:T(8,128)(2,1)} %v_hbm.1, s32[1,2]{1,0:T(1,128)} %order_hbm.1, f32[16,128]{1,0:T(8,128)} %bitcast.1), custom_call_target="tpu_custom_call" | custom-call | tf_op jit(solution)/shard_map/pallas_call | solution.py:232
  58.6 1.5 %copy.7 = bf16[640,2048]{1,0:T(8,128)(2,1)} copy(bf16[640,2048]{1,0:T(8,128)(2,1)S(1)} %shard_map.55) | data formatting | bytes 5242880
